TPU v7x, 768 devices: a whole 4x8x12 slice. The times are simulated.
768 devices in a mesh: stretch: 128 (over x, z_lo, y), col: 6 (over z_hi, core).
Axes of the slice: x: 4, y: 8, z: 12 (z_hi: 3, z_lo: 4; z = z_hi * 4 + z_lo), core: 2. Of those that a mesh axis runs over, the one named last changes fastest.
Arguments:
- queries: bfloat16 [16384, 1536], P('stretch', 'col'), may hold values from -32 to 32
- keys: bfloat16 [16384, 1536], P('stretch', 'col'), may hold values from -32 to 32
- values: bfloat16 [16384, 1536], P('stretch', 'col'), may hold values from -6 to 6
- memory_first: bfloat16 [12, 128, 256], P('col'), may hold values from -0.5 to 0.5
- memory_second_weight: bfloat16 [12, 256, 128], P('col'), may hold values from -0.375 to 0.375
- out_weight: bfloat16 [1536, 2048], P('col'), may hold values from -0.15625 to 0.15625
- decay: float32 [128, 12, 256], P('stretch', 'col'), may hold values from 0.05 to 1
- boundary: int32 [128], P('stretch'), may hold values from 0 to 1
- win_blocks: int32 [12], P('col'), may hold values from 1 to 4
Outputs:
- attention_out: bfloat16 [16384, 1536], P('stretch', 'col')
- memory_out: bfloat16 [16384, 2048], P('stretch')
All inputs are finite; a program needn't handle non-finite values.
Results may differ from a plain program's by a relative error of at most 0.017.
Values may be sent and summed in bfloat16 or wider, within the bound.
A program may use at most 192 MiB of HBM per device.

v0:
```python
import math

import jax
import jax.numpy as jnp
from jax import lax
from jax.sharding import PartitionSpec as P

HD = 128
TOK_DEV = 128
WMAX = 4


def passed_along(value, axis, steps):
    count = lax.axis_size(axis)
    leading, last = (max(0, -steps), min(count, count - steps))
    return lax.ppermute(value, axis, [(source, source + steps) for source in range(leading, last)])


def entering(shard, axis, combine, identity):
    size, place = (lax.axis_size(axis), lax.axis_index(axis))
    everything = jax.tree.map(lambda part: lax.all_gather(part, axis), shard)
    start = jax.tree.map(
        lambda part, zero: jnp.broadcast_to(jnp.asarray(zero, part.dtype), part.shape),
        shard,
        identity,
    )

    def step(k, before):
        reached = k < place
        new = combine(before, jax.tree.map(lambda part: part[k], everything))
        return jax.tree.map(lambda a, b: jnp.where(reached, a, b), new, before)

    return lax.fori_loop(0, size, step, start)


def silu_slope(z):
    sig = jax.nn.sigmoid(z)
    return sig * (1.0 + z * (1.0 - sig))


def join_both(earlier, later):
    return (
        earlier[0] * later[0],
        earlier[1] * later[0][:, None, :] + later[1],
        earlier[2] * later[0][:, :, None] + later[2],
    )


def shards(
    queries,
    keys,
    values,
    memory_first,
    memory_second_weight,
    out_weight,
    decay,
    boundary,
    win_blocks,
):
    tok_rows = keys.shape[0]
    heads_here = win_blocks.shape[0]
    width = heads_here * HD
    own_flag = boundary.astype(jnp.bfloat16)
    pair = jnp.stack([keys, values])
    received = [(pair, own_flag)]
    current = (pair, own_flag)
    for step in range(WMAX):
        current = passed_along((current[0], current[1]), "stretch", 1)
        received.append(current)
    position = lax.axis_index("stretch")
    clear = jnp.ones((), jnp.float32)
    block_ok = [jnp.ones((heads_here,), jnp.float32)]
    for step in range(1, WMAX + 1):
        clear = clear * (1.0 - received[step - 1][1][0].astype(jnp.float32))
        inside = (position >= step).astype(jnp.float32)
        within = (win_blocks >= step).astype(jnp.float32)
        block_ok.append(clear * inside * within)
    ordered = received[::-1]
    key_rows = jnp.concatenate([item[0][0] for item in ordered], 0).reshape(-1, heads_here, HD)
    value_rows = jnp.concatenate([item[0][1] for item in ordered], 0).reshape(-1, heads_here, HD)
    allowed_blocks = jnp.stack(block_ok[::-1], 1)
    allowed = jnp.repeat(allowed_blocks, tok_rows, axis=1) > 0.5
    span = (WMAX + 1) * tok_rows
    key_local = jnp.arange(span) - WMAX * tok_rows
    causal = key_local[None, :] <= jnp.arange(tok_rows)[:, None]
    mask = allowed[:, None, :] & causal[None, :, :]
    q3 = queries.reshape(tok_rows, heads_here, HD)
    scores = jnp.einsum("qhd,khd->hqk", q3, key_rows, preferred_element_type=jnp.float32) * (
        1.0 / math.sqrt(HD)
    )
    scores = jnp.where(mask, scores, -1e30)
    top = jnp.max(scores, axis=-1, keepdims=True)
    expo = jnp.exp(scores - top)
    weights = (expo / jnp.sum(expo, axis=-1, keepdims=True)).astype(jnp.bfloat16)
    attended = jnp.einsum("hqk,khd->qhd", weights, value_rows, preferred_element_type=jnp.float32)
    attention_out = attended.astype(jnp.bfloat16).reshape(tok_rows, width)
    eta = 1.0 / (TOK_DEV * math.sqrt(lax.axis_size("stretch")))
    k3 = keys.reshape(tok_rows, heads_here, HD)
    v3 = values.reshape(tok_rows, heads_here, HD)
    z = jnp.einsum("thd,hdm->htm", k3, memory_first, preferred_element_type=jnp.float32)
    hidden_units = jax.nn.silu(z).astype(jnp.bfloat16)
    memory_prediction = jnp.einsum(
        "pof,pfk->opk", hidden_units, memory_second_weight, preferred_element_type=jnp.float32
    )
    error_signal = (memory_prediction - v3.astype(jnp.float32)).astype(jnp.bfloat16)
    gradient_second_layer = jnp.einsum(
        "qzu,zqs->qus", hidden_units, error_signal, preferred_element_type=jnp.float32
    )
    backward_pass = jnp.einsum(
        "lun,uon->ulo", error_signal, memory_second_weight, preferred_element_type=jnp.float32
    )
    dz = (backward_pass * silu_slope(z)).astype(jnp.bfloat16)
    grad_first = jnp.einsum("thd,htm->hdm", k3, dz, preferred_element_type=jnp.float32)
    keep = decay[0] * (1 - boundary[0]).astype(jnp.float32)
    update_first = -eta * grad_first
    update_second = -eta * gradient_second_layer
    ones_keep = jnp.ones_like(keep)
    before = entering(
        (keep, update_first, update_second),
        "stretch",
        join_both,
        (ones_keep, jnp.zeros_like(update_first), jnp.zeros_like(update_second)),
    )
    state_first = before[1] * keep[:, None, :] + update_first
    state_second = before[2] * keep[:, :, None] + update_second
    fast_first = (memory_first.astype(jnp.float32) + state_first).astype(jnp.bfloat16)
    memory_recall = jax.nn.silu(
        jnp.einsum("thd,hdm->thm", q3, fast_first, preferred_element_type=jnp.float32)
    ).astype(jnp.bfloat16)
    quick_second_layer = (memory_second_weight.astype(jnp.float32) + state_second).astype(
        jnp.bfloat16
    )
    memory_readout = jnp.einsum(
        "flp,lpe->fle", memory_recall, quick_second_layer, preferred_element_type=jnp.float32
    ).astype(jnp.bfloat16)
    partial_out = jnp.dot(
        memory_readout.reshape(tok_rows, width), out_weight, preferred_element_type=jnp.float32
    )
    group_term = partial_out.astype(jnp.bfloat16)
    memory_out = lax.psum(group_term, "col").astype(jnp.float32).astype(jnp.bfloat16)
    return (attention_out, memory_out)


def solution(mesh):
    placed = (
        P("stretch", "col"),
        P("stretch", "col"),
        P("stretch", "col"),
        P("col", None, None),
        P("col", None, None),
        P("col", None),
        P("stretch", "col", None),
        P("stretch"),
        P("col"),
    )
    return jax.shard_map(
        shards,
        mesh=mesh,
        in_specs=placed,
        out_specs=(P("stretch", "col"), P("stretch", None)),
        check_vma=False,
    )
```

profile of v0, /device:TPU:1, one launch (start us, length us, event | category | flops | bytes accessed | tf_op | source)
XLA Modules:
  0.0 1919.6 jit_solution(18121411652473930596)
XLA Ops:
  10.4 1.2 fusion.10
  11.5 1.3 fusion.7
  15.5 4.7 collective-permute-start.4
  20.2 3.2 collective-permute-start
  25.4 320.7 %all_gather.16 = f32[128,2,256]{2,1,0:T(2,128)S(1)} all-gather(f32[1,2,256]{2,1,0:T(2,128)S(1)} %broadcast_multiply_fusion), channel_id=1, replica_groups=mesh['stretch'=128,'col'=6] {'stretch'}, dimensions={0}, use_global_device_ids=true | all-gather | bytes 264192 | tf_op jit(solution)/shard_map/all_gather | solution.py:21
  346.1 1.3 fusion.58
  348.2 1.8 collective-permute-start.5
  350.8 4.5 collective-permute-start.6
  358.0 3.5 collective-permute-start.1
  361.7 4.4 collective-permute-done.1
  366.1 4.2 collective-permute-start.2
  370.4 2.1 collective-permute-done.2
  372.5 3.8 collective-permute-start.3
  376.5 4.1 collective-permute-done.3
  380.9 1.3 fusion.41
  382.2 314.3 %all-gather.5.cloned.1.call-done = f32[256,128,256]{2,1,0:T(8,128)} async-done(((f32[2,128,256]{2,1,0:T(8,128)}), f32[256,128,256]{2,1,0:T(8,128)}) %all-gather.5.cloned.1.call-update) | async-done | bytes 33554448 | tf_op jit(solution)/shard_map/all_gather | solution.py:21
  696.5 752.7 %all-gather.7.cloned.1.call-done = f32[256,256,128]{2,1,0:T(8,128)} async-done(((f32[2,256,128]{2,1,0:T(8,128)}), f32[256,256,128]{2,1,0:T(8,128)}) %all-gather.7.cloned.1.call-update) | async-done | bytes 33554448 | tf_op jit(solution)/shard_map/all_gather | solution.py:21
  1449.2 291.9 %while.16 = (s32[]{:T(128)}, f32[2,128,256]{2,1,0:T(8,128)S(1)}, f32[2,256,128]{2,1,0:T(8,128)S(1)}, s32[]{:T(128)}, f32[128,2,256]{2,1,0:T(2,128)S(1)}, /*index...) while((s32[]{:T(128)}, f32[2,128,256]{2,1,0:T(8,128)S(1)}, ...), condition=%wide.region_3.4_spmd.clone, body=%wide.region_2.3_spmd.clone.sunk | while | flops 524292 | bytes 1581183 | solution.py:33
  1451.5 1.1 fusion.65
  1458.3 1.1 fusion.65
  1462.9 1.1 fusion.65
  1469.7 1.1 fusion.65
  1476.6 1.1 fusion.65
  1483.4 1.1 fusion.65
  1488.0 1.1 fusion.65
  1494.8 1.1 fusion.65
  1501.7 1.1 fusion.65
  1506.2 1.1 fusion.65
  1513.1 1.1 fusion.65
  1519.9 1.1 fusion.65
  1526.8 1.1 fusion.65
  1531.3 1.1 fusion.65
  1538.2 1.1 fusion.65
  1545.0 1.1 fusion.65
  1549.6 1.1 fusion.65
  1556.4 1.1 fusion.65
  1563.3 1.1 fusion.65
  1570.1 1.1 fusion.65
  1574.7 1.1 fusion.65
  1581.5 1.1 fusion.65
  1588.3 1.1 fusion.65
  1592.9 1.1 fusion.65
  1599.8 1.1 fusion.65
  1606.6 1.1 fusion.65
  1613.4 1.1 fusion.65
  1618.0 1.1 fusion.65
  1624.8 1.1 fusion.65
  1631.7 1.1 fusion.65
  1636.2 1.1 fusion.65
  1643.1 1.1 fusion.65
  1649.9 1.1 fusion.65
  1656.8 1.1 fusion.65
  1661.3 1.1 fusion.65
  1668.2 1.1 fusion.65
  1675.0 1.1 fusion.65
  1679.6 1.1 fusion.65
  1686.4 1.1 fusion.65
  1693.3 1.1 fusion.65
  1700.1 1.1 fusion.65
  1704.7 1.1 fusion.65
  1711.5 1.1 fusion.65
  1741.3 1.5 convolution_convert_fusion.2
  1746.2 165.0 %all-reduce.2.cloned.1.call-done = bf16[128,2048]{1,0:T(8,128)(2,1)} async-done(((bf16[128,2048]{1,0:T(8,128)(2,1)}), bf16[128,2048]{1,0:T(8,128)(2,1)}) %all-reduce.2.cloned.1.call-update) | async-done | bytes 524304 | tf_op jit(solution)/shard_map/psum | solution.py:140
  1911.2 1.9 copy.130
  (399 shorter events, 251.1 us)
Async XLA Ops:
  7.2 1735.6 %copy-start = (bf16[256,2048]{1,0:T(8,128)(2,1)S(1)}, bf16[256,2048]{1,0:T(8,128)(2,1)}, u32[]{:S(2)}) copy-start(bf16[256,2048]{1,0:T(8,128)(2,1)} %param.16) | copy-start | bytes 3145732
  7.2 689.3 %all-gather.5.cloned.1.call-start = ((), (), s32[]{:S(2)}) async-start(), calls=%async_computation.1 | async-start | bytes 33816576 | tf_op jit(solution)/shard_map/all_gather | solution.py:21
  13.7 1435.5 %all-gather.7.cloned.1.call-start = ((), (), s32[]{:S(2)}) async-start(), calls=%async_computation.2 | async-start | bytes 33816576 | tf_op jit(solution)/shard_map/all_gather | solution.py:21
  14.8 1896.4 %all-reduce.2.cloned.1.call-start = ((), (), s32[]{:S(2)}) async-start(), calls=%async_computation | async-start | bytes 1048576 | tf_op jit(solution)/shard_map/psum | solution.py:140
  15.5 332.0 %collective-permute-start.4 = (bf16[1]{0:T(256)(128)(2,1)}, bf16[1]{0:T(256)(128)(2,1)}, u32[]{:S(2)}, u32[]{:S(2)}) collective-permute-start(bf16[1]{0:T(256)(128)(2,1)} %convert_element_type.80), channel_id=1, source_target_pairs={{0,6},{6,12},{12,18},{18,24},{24,30},{30,36},{36,42},{42,48},{48,5... | collective-permute-start | bytes 14 | tf_op jit(solution)/shard_map/ppermute | solution.py:16
  20.2 337.8 %collective-permute-start = (bf16[2,128,256]{1,2,0:T(8,128)(2,1)S(1)}, bf16[2,128,256]{1,2,0:T(8,128)(2,1)S(1)}, u32[]{:S(2)}, u32[]{:S(2)}) collective-permute-start(bf16[2,128,256]{1,2,0:T(8,128)(2,1)S(1)} %pad_maximum_fusion), channel_id=1, source_target_pairs={{0,6},{6,12},{12,18},{18,24},{24,30},{30,36},{36,42},{42,48},{48,5... | collective-permute-start | bytes 393224 | tf_op jit(solution)/shard_map/ppermute | solution.py:16
  348.2 2.1 collective-permute-start.5
  350.8 4.7 collective-permute-start.6
  358.0 8.0 collective-permute-start.1
  366.1 6.5 collective-permute-start.2
  372.5 8.0 collective-permute-start.3
Sparse Core Ops, SparseCore 0:
  13.8 682.5 all-gather.4
  699.4 749.7 all-gather.6
  1744.0 167.1 all-reduce.1
where the time goes:
time: 1930 us; the launch traced here: 1920 us
  waiting for transfers between devices  1240 us (64%)
  blocking collectives  321 us (17%)
  other arithmetic  289 us (15%)
  starting transfers between devices  25.9 us (1%)
    all_gather x2, waiting for transfers between devices, entering(): everything = jax.tree.map(lambda part: lax.all_gather(part, axis), shard)  1070 us
    all_gather x1, blocking collectives, entering(): everything = jax.tree.map(lambda part: lax.all_gather(part, axis), shard)  321 us
    select_n x256, other arithmetic, step(): return jax.tree.map(lambda a, b: jnp.where(reached, a, b), new, before)  286 us
    psum x1, waiting for transfers between devices, shards(): lax.psum(group_term, 'col').astype(jnp.float32).astype(jnp.bfloat16)  165 us
  transfers between devices with their start and end apart: 10, of which 8 were waited for; matrix products, arithmetic and copies ran while one was open for 1% of the time, Pallas kernels for 0%

commit v1 on v0

v1 whole, which is shorter than its diff:
```python
import functools
import math

import jax
import jax.numpy as jnp
from jax import lax
from jax.experimental import pallas as pl
from jax.experimental.pallas import tpu as pltpu
from jax.sharding import PartitionSpec as P

HD = 128
MEM = 256
WMAX = 4
NY = 8
LANES = 128
SUB = 8
OUT_COLS = 512
MESH = pl.DeviceIdType.MESH
BF16 = jnp.bfloat16
F32 = jnp.float32


def dot(a, b, ca, cb):
    return lax.dot_general(a, b, (((ca,), (cb,)), ((), ())), preferred_element_type=F32)


def kernel(
    n_stretch,
    n_col,
    q_ref,
    k_ref,
    v_ref,
    m1_ref,
    m2_ref,
    wo_ref,
    decay_ref,
    bnd_ref,
    win_ref,
    att_ref,
    out_ref,
    halo,
    keeps,
    upd,
    cut,
    got,
    inner,
    tot,
    rows_in,
    ent,
    ent_in,
    back,
    back_in,
    wall,
    reads,
    part,
    part_in,
    halo_s,
    halo_r,
    keep_s,
    keep_r,
    cut_s,
    cut_r,
    tot_s,
    tot_r,
    ent_s,
    ent_r,
    back_s,
    back_r,
    wall_s,
    wall_r,
    wall_l,
    read_s,
    read_r,
    part_s,
    part_r,
):
    nr = n_stretch // NY
    groups = n_col // 2
    sr = HD // NY
    dh_n = sr // SUB
    tps = 4 * dh_n * 2 // nr
    n_out = out_ref.shape[1] // OUT_COLS

    pos = lax.axis_index("stretch")
    col = lax.axis_index("col")
    y = lax.rem(pos, NY)
    r = pos // NY
    zh = col // 2
    core = lax.rem(col, 2)
    after = lax.rem(pos + 1, n_stretch)
    before = lax.rem(pos + n_stretch - 1, n_stretch)
    sibling = col + 1 - 2 * core

    def at(s, c):
        return {"stretch": s, "col": c}

    def in_row(i):
        return lax.rem(y + i, NY)

    def in_rows(i):
        return lax.rem(r + i, nr)

    def remote(src, dst, send, recv, where):
        return pltpu.make_async_remote_copy(
            src_ref=src, dst_ref=dst, send_sem=send, recv_sem=recv, device_id=where, device_id_type=MESH
        )

    barrier = pltpu.get_barrier_semaphore()

    def greet(where):
        pl.semaphore_signal(barrier, inc=1, device_id=where, device_id_type=MESH)

    for i in range(1, NY):
        greet(at(r * NY + in_row(i), col))
    for i in range(1, nr):
        greet(at(in_rows(i) * NY + y, col))
    greet(at(after, col))
    greet(at(before, col))
    for g in range(1, groups):
        greet(at(pos, lax.rem(col + 2 * g, n_col)))
    greet(at(pos, sibling))
    greeted = (NY - 1) + (nr - 1) + 2 + (groups - 1) + 1

    own_w = pltpu.make_async_copy(wo_ref, wall.at[zh], wall_l)
    own_w.start()
    flag = bnd_ref[0].astype(F32)
    keep2 = decay_ref[0] * (1.0 - flag)
    keeps[y] = jnp.concatenate([keep2, jnp.zeros((SUB - 2, MEM), F32)], 0)
    halo[0, 0:HD, :] = k_ref[...]
    halo[0, HD : 2 * HD, :] = v_ref[...]
    halo[0, 2 * HD :, :] = jnp.full((16, 2 * HD), flag, F32).astype(BF16)

    eta = 1.0 / (HD * math.sqrt(n_stretch))
    for h in range(2):
        cols = slice(h * HD, (h + 1) * HD)
        kh = k_ref[:, cols]
        m2 = m2_ref[h]
        z = dot(kh, m1_ref[h], 1, 0)
        sig = jax.nn.sigmoid(z)
        hidden = (z * sig).astype(BF16)
        err = (dot(hidden, m2, 1, 0) - v_ref[:, cols].astype(F32)).astype(BF16)
        dz = (dot(err, m2, 1, 1) * (sig * (1.0 + z * (1.0 - sig)))).astype(BF16)
        for layer, grad in enumerate((dot(kh, dz, 0, 0), dot(err, hidden, 0, 0))):
            u = -eta * grad
            upd[2 * h + layer] = u
            for s in range(NY):
                cut[s, 2 * h + layer] = u[s * sr : (s + 1) * sr].astype(BF16)
    got[y] = cut[y]

    pl.semaphore_wait(barrier, greeted)

    def keep_copy(i):
        to = in_row(i)
        return remote(keeps.at[y], keeps.at[y], keep_s.at[to], keep_r.at[y], at(r * NY + to, col))

    def cut_copy(i):
        to = in_row(i)
        return remote(cut.at[to], got.at[y], cut_s.at[to], cut_r.at[y], at(r * NY + to, col))

    def halo_copy(k):
        return remote(halo.at[k], halo.at[k + 1], halo_s.at[k], halo_r.at[k + 1], at(after, col))

    def wall_copy(g):
        return remote(wo_ref, wall.at[zh], wall_s.at[g], wall_r.at[zh], at(pos, lax.rem(col + 2 * g, n_col)))

    for i in range(1, NY):
        keep_copy(i).start()
    for i in range(1, NY):
        cut_copy(i).start()
    halo_copy(0).start()
    for g in range(1, groups):
        wall_copy(g).start()

    for i in range(1, NY):
        o = in_row(i)
        remote(keeps.at[o], keeps.at[o], keep_s.at[o], keep_r.at[o], at(pos, col)).wait_recv()
        remote(cut.at[o], got.at[o], cut_s.at[o], cut_r.at[o], at(pos, col)).wait_recv()
    run = [jnp.zeros((sr, MEM), F32) for _ in range(4)]
    decayed = [jnp.ones((1, MEM), F32) for _ in range(2)]
    decayed_at = []
    for b in range(NY):
        decayed_at.append(list(decayed))
        for h in range(2):
            kb = keeps[b, h : h + 1, :]
            for hl in (2 * h, 2 * h + 1):
                inner[b, hl] = run[hl]
                run[hl] = run[hl] * kb + got[b, hl].astype(F32)
            decayed[h] = decayed[h] * kb

    def tiles():
        t = 0
        for hl in range(4):
            for dh in range(dh_n):
                for jh in range(2):
                    yield t // tps, t % tps, hl, slice(dh * SUB, (dh + 1) * SUB), slice(jh * LANES, (jh + 1) * LANES)
                    t += 1

    for owner, slot, hl, ds_, js in tiles():
        tot[owner, slot, 0] = run[hl][ds_, js]
        tot[owner, slot, 1] = jnp.broadcast_to(decayed[hl // 2][:, js], (SUB, LANES))
    rows_in[r] = tot[r]

    def tot_copy(i):
        to = in_rows(i)
        return remote(tot.at[to], rows_in.at[r], tot_s.at[to], tot_r.at[r], at(to * NY + y, col))

    for i in range(1, nr):
        tot_copy(i).start()

    def halo_got(k):
        remote(halo.at[k - 1], halo.at[k], halo_s.at[k - 1], halo_r.at[k], at(pos, col)).wait_recv()

    halo_got(1)
    halo_copy(1).start()

    for i in range(1, nr):
        o = in_rows(i)
        remote(tot.at[o], rows_in.at[o], tot_s.at[o], tot_r.at[o], at(pos, col)).wait_recv()
    for slot in range(tps):
        e = jnp.zeros((SUB, LANES), F32)
        for rr in range(nr):
            ent[rr, slot] = e
            e = e * rows_in[rr, slot, 1] + rows_in[rr, slot, 0]
    ent_in[r] = ent[r]

    def ent_copy(i):
        to = in_rows(i)
        return remote(ent.at[to], ent_in.at[r], ent_s.at[to], ent_r.at[r], at(to * NY + y, col))

    for i in range(1, nr):
        ent_copy(i).start()

    halo_got(2)
    halo_copy(2).start()

    for i in range(1, nr):
        o = in_rows(i)
        remote(ent.at[o], ent_in.at[o], ent_s.at[o], ent_r.at[o], at(pos, col)).wait_recv()
    for owner, slot, hl, ds_, js in tiles():
        e = ent_in[owner, slot]
        for b in range(NY):
            whole = inner[b, hl, ds_, js] + e * decayed_at[b][hl // 2][:, js]
            inner[b, hl, ds_, js] = whole
    for b in range(NY):
        for hl in range(4):
            back[b, hl] = inner[b, hl].astype(BF16)
    back_in[y] = back[y]

    def back_copy(i):
        to = in_row(i)
        return remote(back.at[to], back_in.at[y], back_s.at[to], back_r.at[y], at(r * NY + to, col))

    for i in range(1, NY):
        back_copy(i).start()

    halo_got(3)
    halo_copy(3).start()

    for i in range(1, NY):
        o = in_row(i)
        remote(back.at[o], back_in.at[o], back_s.at[o], back_r.at[o], at(pos, col)).wait_recv()
    read = []
    for h in range(2):
        kh = keep2[h : h + 1, :]
        state = []
        for layer in range(2):
            hl = 2 * h + layer
            entering = jnp.concatenate([back_in[s, hl] for s in range(NY)], 0).astype(F32)
            state.append(entering * kh + upd[hl])
        fast_first = (m1_ref[h].astype(F32) + state[0]).astype(BF16)
        fast_second = (m2_ref[h].astype(F32).T + state[1]).astype(BF16)
        zq = dot(q_ref[:, h * HD : (h + 1) * HD], fast_first, 1, 0)
        recall = (zq * jax.nn.sigmoid(zq)).astype(BF16)
        read.append(dot(recall, fast_second, 1, 1).astype(BF16))
    reads[zh] = jnp.concatenate(read, 1)

    def read_copy(g):
        return remote(
            reads.at[zh], reads.at[zh], read_s.at[g], read_r.at[zh], at(pos, lax.rem(col + 2 * g, n_col))
        )

    for g in range(1, groups):
        read_copy(g).start()

    halo_got(4)
    scale = 1.0 / math.sqrt(HD)
    causal = lax.broadcasted_iota(jnp.int32, (HD, HD), 1) <= lax.broadcasted_iota(jnp.int32, (HD, HD), 0)
    clear = jnp.ones((1, HD), F32)
    clear_at = []
    for k in range(1, WMAX + 1):
        clear = clear * (1.0 - halo[k - 1, 2 * HD : 2 * HD + 16, 0:HD].astype(F32)[0:1])
        clear_at.append(clear * jnp.where(pos >= k, 1.0, 0.0))
    for h in range(2):
        cols = slice(h * HD, (h + 1) * HD)
        qh = q_ref[:, cols]
        s = [jnp.where(causal, dot(qh, halo[0, 0:HD, cols], 1, 1) * scale, -1e30)]
        for k in range(1, WMAX + 1):
            ok = clear_at[k - 1] * jnp.where(win_ref[h] >= k, 1.0, 0.0)
            s.append(jnp.where(ok > 0.5, dot(qh, halo[k, 0:HD, cols], 1, 1) * scale, -1e30))
        s = jnp.concatenate(s, 1)
        top = jnp.max(s, axis=1, keepdims=True)
        e = jnp.exp(s - top)
        w = (e / jnp.sum(e, axis=1, keepdims=True)).astype(BF16)
        vals = jnp.concatenate([halo[k, HD : 2 * HD, cols] for k in range(WMAX + 1)], 0)
        att_ref[:, cols] = dot(w, vals, 1, 0).astype(BF16)

    own_w.wait()
    for g in range(1, groups):
        o = lax.rem(zh + g, groups)
        remote(wo_ref, wall.at[o], wall_s.at[g], wall_r.at[o], at(pos, col)).wait_recv()
        remote(reads.at[o], reads.at[o], read_s.at[g], read_r.at[o], at(pos, col)).wait_recv()
    left = jnp.concatenate([reads[g] for g in range(groups)], 1)

    def part_copy(c):
        return remote(part.at[c], part_in.at[c], part_s.at[c], part_r.at[c], at(pos, sibling))

    for c in range(n_out):
        cs = slice(c * OUT_COLS, (c + 1) * OUT_COLS)
        right = jnp.concatenate([wall[g, :, cs] for g in range(groups)], 0)
        part[c] = dot(left, right, 1, 0).astype(BF16)
        part_copy(c).start()
    for c in range(n_out):
        cs = slice(c * OUT_COLS, (c + 1) * OUT_COLS)
        part_copy(c).wait_recv()
        out_ref[:, cs] = (part[c].astype(F32) + part_in[c].astype(F32)).astype(BF16)

    for i in range(1, NY):
        keep_copy(i).wait_send()
        cut_copy(i).wait_send()
        back_copy(i).wait_send()
    for i in range(1, nr):
        tot_copy(i).wait_send()
        ent_copy(i).wait_send()
    for k in range(WMAX):
        halo_copy(k).wait_send()
    for g in range(1, groups):
        wall_copy(g).wait_send()
        read_copy(g).wait_send()
    for c in range(n_out):
        part_copy(c).wait_send()


def solution(mesh):
    n_stretch, n_col = mesh.shape["stretch"], mesh.shape["col"]
    nr, groups, sr = n_stretch // NY, n_col // 2, HD // NY
    tps = 4 * (sr // SUB) * 2 // nr

    def shards(queries, keys, values, memory_first, memory_second_weight, out_weight, decay, boundary, win_blocks):
        d = out_weight.shape[1]
        vmem = pl.BlockSpec(memory_space=pltpu.VMEM)
        smem = pl.BlockSpec(memory_space=pltpu.SMEM)
        dma = pltpu.SemaphoreType.DMA
        return tuple(
            pl.pallas_call(
                functools.partial(kernel, n_stretch, n_col),
                out_shape=(
                    jax.ShapeDtypeStruct((HD, 2 * HD), BF16),
                    jax.ShapeDtypeStruct((HD, d), BF16),
                ),
                in_specs=[vmem] * 5 + [pl.BlockSpec(memory_space=pl.ANY)] + [vmem, smem, smem],
                out_specs=(vmem, vmem),
                scratch_shapes=[
                    pltpu.VMEM((WMAX + 1, 2 * HD + 16, 2 * HD), BF16),
                    pltpu.VMEM((NY, SUB, MEM), F32),
                    pltpu.VMEM((4, HD, MEM), F32),
                    pltpu.VMEM((NY, 4, sr, MEM), BF16),
                    pltpu.VMEM((NY, 4, sr, MEM), BF16),
                    pltpu.VMEM((NY, 4, sr, MEM), F32),
                    pltpu.VMEM((nr, tps, 2, SUB, LANES), F32),
                    pltpu.VMEM((nr, tps, 2, SUB, LANES), F32),
                    pltpu.VMEM((nr, tps, SUB, LANES), F32),
                    pltpu.VMEM((nr, tps, SUB, LANES), F32),
                    pltpu.VMEM((NY, 4, sr, MEM), BF16),
                    pltpu.VMEM((NY, 4, sr, MEM), BF16),
                    pltpu.VMEM((groups, 2 * HD, d), BF16),
                    pltpu.VMEM((groups, HD, 2 * HD), BF16),
                    pltpu.VMEM((d // OUT_COLS, HD, OUT_COLS), BF16),
                    pltpu.VMEM((d // OUT_COLS, HD, OUT_COLS), BF16),
                    dma((WMAX + 1,)),
                    dma((WMAX + 1,)),
                    dma((NY,)),
                    dma((NY,)),
                    dma((NY,)),
                    dma((NY,)),
                    dma((nr,)),
                    dma((nr,)),
                    dma((nr,)),
                    dma((nr,)),
                    dma((NY,)),
                    dma((NY,)),
                    dma((groups,)),
                    dma((groups,)),
                    dma,
                    dma((groups,)),
                    dma((groups,)),
                    dma((d // OUT_COLS,)),
                    dma((d // OUT_COLS,)),
                ],
                compiler_params=pltpu.CompilerParams(
                    collective_id=0, has_side_effects=True, vmem_limit_bytes=48 * 2**20
                ),
            )(
                queries,
                keys,
                values,
                memory_first,
                memory_second_weight,
                out_weight,
                decay,
                boundary,
                win_blocks,
            )
        )

    placed = (
        P("stretch", "col"),
        P("stretch", "col"),
        P("stretch", "col"),
        P("col", None, None),
        P("col", None, None),
        P("col", None),
        P("stretch", "col", None),
        P("stretch"),
        P("col"),
    )
    return jax.shard_map(
        shards,
        mesh=mesh,
        in_specs=placed,
        out_specs=(P("stretch", "col"), P("stretch", None)),
        check_vma=False,
    )
```

time: 1930 us -> 154 us (0.08)
  waiting for transfers between devices: 1240 us -> 0 us
  blocking collectives: 321 us -> 0 us
  other arithmetic: 289 us -> 0 us
  Pallas kernels: 0 us -> 144 us
  starting transfers between devices: 25.9 us -> 0 us
    all_gather x2 -> x0, waiting for transfers between devices: 1070 us -> none  [entering(): everything = jax.tree.map(lambda part: lax.all_gather(part, axis), shard)]
    all_gather x1 -> x0, blocking collectives: 321 us -> none  [entering(): everything = jax.tree.map(lambda part: lax.all_gather(part, axis), shard)]
    select_n x256 -> x0, other arithmetic: 286 us -> none  [step(): return jax.tree.map(lambda a, b: jnp.where(reached, a, b), new, before)]
    psum x1 -> x0, waiting for transfers between devices: 165 us -> none  [shards(): lax.psum(group_term, 'col').astype(jnp.float32).astype(jnp.bfloat16)]
    pallas_call x0 -> x1, Pallas kernels: none -> 144 us  [shards(): pl.pallas_call(functools.partial(kernel, n_stretch, n_col), out_shape=(ja...]
    ppermute x7 -> x0, starting transfers between devices: 25.8 us -> none  [passed_along(): lax.ppermute(value, axis, [(source, source + steps) for source in range(l...]
  transfers between devices with their start and end apart: 10 -> 0, of which waited for: 8 -> 0; matrix products, arithmetic and copies ran while one was open for 1% -> 0% of each run, Pallas kernels for 0% -> 0%
where the time goes in v1:
time: 154 us; the launch traced here: 153 us
  Pallas kernels  144 us (94%)
  local copies, waits for them, and re-layouts  7.65 us (5%)
    pallas_call x1, Pallas kernels, shards(): pl.pallas_call(functools.partial(kernel, n_stretch, n_col), out_shape=(ja...  144 us
    unnamed x18, local copies, waits for them, and re-layouts  7.65 us

profile of v1, /device:TPU:1, one launch (start us, length us, event | category | flops | bytes accessed | tf_op | source)
XLA Modules:
  0.0 153.1 jit_solution(9705955330530005478)
XLA Ops:
  0.6 0.0 copy-start.7
  1.3 0.0 copy-done.7
  1.3 0.0 copy-start
  1.3 1.2 copy-done
  2.5 0.0 copy-start.1
  2.5 0.9 copy-done.1
  3.4 0.0 copy-start.2
  3.4 0.9 copy-done.2
  4.3 0.0 copy-start.3
  4.3 0.8 copy-done.3
  5.2 0.0 copy-start.4
  5.2 0.8 copy-done.4
  6.0 0.0 copy-start.5
  6.0 0.8 copy-done.5
  6.9 0.0 copy-start.6
  6.9 0.7 copy-done.6
  7.5 144.1 %shard_map.104 = (bf16[128,256]{1,0:T(8,128)(2,1)S(1)}, bf16[128,2048]{1,0:T(8,128)(2,1)S(1)}) custom-call(bf16[128,256]{1,0:T(8,128)(2,1)S(1)} %copy-done.3, bf16[128,256]{1,0:T(8,128)(2,1)S(1)} %copy-done.4, bf16[128,256]{1,0:T(8,128)(2,1)S(1)} %copy-done.5, bf16[2,128,256]{2,1,0:T(8,128)(2,1)S(1)} %copy-done.1, bf16[2,256,128]{2,1,0:T(8,128)(2,1)S(1)} %copy-done.2, ...), custom_call_target="tpu_custom_call" | custom-call | tf_op jit(solution)/shard_map/pallas_call | solution.py:354
  151.7 0.6 copy.14
  152.3 0.8 copy.15
Async XLA Ops:
  0.6 0.7 copy-start.7
  1.3 1.2 copy-start
  2.5 0.9 copy-start.1
  3.4 0.9 copy-start.2
  4.3 0.8 copy-start.3
  5.2 0.8 copy-start.4
  6.0 0.8 copy-start.5
  6.9 0.7 copy-start.6

commit v2 on v1

--- a/solution.py
+++ b/solution.py
@@ -12,6 +12,8 @@
 MEM = 256
 WMAX = 4
 NY = 8
+NZ = 4
+CHUNKS = 8
 LANES = 128
 SUB = 8
 OUT_COLS = 512
@@ -27,17 +29,21 @@
 def kernel(
     n_stretch,
     n_col,
-    q_ref,
-    k_ref,
-    v_ref,
-    m1_ref,
-    m2_ref,
+    q_hbm,
+    k_hbm,
+    v_hbm,
+    m1_hbm,
+    m2_hbm,
     wo_ref,
-    decay_ref,
+    decay_hbm,
     bnd_ref,
     win_ref,
     att_ref,
     out_ref,
+    q_ref,
+    m1_ref,
+    m2_ref,
+    decay_ref,
     halo,
     keeps,
     upd,
@@ -54,6 +60,7 @@
     reads,
     part,
     part_in,
+    in_s,
     halo_s,
     halo_r,
     keep_s,
@@ -66,8 +73,10 @@
     ent_r,
     back_s,
     back_r,
-    wall_s,
-    wall_r,
+    up_s,
+    up_r,
+    down_s,
+    down_r,
     wall_l,
     read_s,
     read_r,
@@ -85,6 +94,7 @@
     col = lax.axis_index("col")
     y = lax.rem(pos, NY)
     r = pos // NY
+    zl = lax.rem(r, NZ)
     zh = col // 2
     core = lax.rem(col, 2)
     after = lax.rem(pos + 1, n_stretch)
@@ -99,6 +109,14 @@
 
     def in_rows(i):
         return lax.rem(r + i, nr)
+
+    ends, starts = zl == NZ - 1, zl == 0
+    above = at(
+        jnp.where(ends, pos - (NZ - 1) * NY, pos + NY), jnp.where(ends, lax.rem(col + 2, n_col), col)
+    )
+    below = at(
+        jnp.where(starts, pos + (NZ - 1) * NY, pos - NY), jnp.where(starts, lax.rem(col + n_col - 2, n_col), col)
+    )
 
     def remote(src, dst, send, recv, where):
         return pltpu.make_async_remote_copy(
@@ -119,26 +137,44 @@
     for g in range(1, groups):
         greet(at(pos, lax.rem(col + 2 * g, n_col)))
     greet(at(pos, sibling))
-    greeted = (NY - 1) + (nr - 1) + 2 + (groups - 1) + 1
-
+    greet(above)
+    greet(below)
+    greeted = (NY - 1) + (nr - 1) + 2 + (groups - 1) + 1 + 2
+
+    own = halo.at[0]
+    loads = [
+        pltpu.make_async_copy(src, dst, in_s.at[i])
+        for i, (src, dst) in enumerate(
+            (
+                (k_hbm, own.at[0:HD]),
+                (m1_hbm, m1_ref),
+                (m2_hbm, m2_ref),
+                (v_hbm, own.at[HD : 2 * HD]),
+                (decay_hbm, decay_ref),
+                (q_hbm, q_ref),
+            )
+        )
+    ]
+    for load in loads:
+        load.start()
     own_w = pltpu.make_async_copy(wo_ref, wall.at[zh], wall_l)
     own_w.start()
     flag = bnd_ref[0].astype(F32)
+    halo[0, 2 * HD :, :] = jnp.full((16, 2 * HD), flag, F32).astype(BF16)
+    for load in loads:
+        load.wait()
     keep2 = decay_ref[0] * (1.0 - flag)
     keeps[y] = jnp.concatenate([keep2, jnp.zeros((SUB - 2, MEM), F32)], 0)
-    halo[0, 0:HD, :] = k_ref[...]
-    halo[0, HD : 2 * HD, :] = v_ref[...]
-    halo[0, 2 * HD :, :] = jnp.full((16, 2 * HD), flag, F32).astype(BF16)
 
     eta = 1.0 / (HD * math.sqrt(n_stretch))
     for h in range(2):
         cols = slice(h * HD, (h + 1) * HD)
-        kh = k_ref[:, cols]
+        kh = halo[0, 0:HD, cols]
         m2 = m2_ref[h]
         z = dot(kh, m1_ref[h], 1, 0)
         sig = jax.nn.sigmoid(z)
         hidden = (z * sig).astype(BF16)
-        err = (dot(hidden, m2, 1, 0) - v_ref[:, cols].astype(F32)).astype(BF16)
+        err = (dot(hidden, m2, 1, 0) - halo[0, HD : 2 * HD, cols].astype(F32)).astype(BF16)
         dz = (dot(err, m2, 1, 1) * (sig * (1.0 + z * (1.0 - sig)))).astype(BF16)
         for layer, grad in enumerate((dot(kh, dz, 0, 0), dot(err, hidden, 0, 0))):
             u = -eta * grad
@@ -160,16 +196,48 @@
     def halo_copy(k):
         return remote(halo.at[k], halo.at[k + 1], halo_s.at[k], halo_r.at[k + 1], at(after, col))
 
-    def wall_copy(g):
-        return remote(wo_ref, wall.at[zh], wall_s.at[g], wall_r.at[zh], at(pos, lax.rem(col + 2 * g, n_col)))
+    rows_c = 2 * HD // CHUNKS
+    wait_g = lax.rem(zh + groups - 1, groups), lax.rem(zh + 1, groups)
+    send_g = jnp.where(ends, zh, wait_g[0]), jnp.where(starts, zh, wait_g[1])
+
+    def wall_copy(way, g, c):
+        piece = wall.at[g, pl.ds(pl.multiple_of(c * rows_c, rows_c), rows_c)]
+        sem_s, sem_r = ((up_s, up_r), (down_s, down_r))[way]
+        return remote(piece, piece, sem_s.at[c], sem_r.at[c], (above, below)[way])
+
+    def pump(j):
+        for way, (d, last) in enumerate(((zl, ends), (NZ - 1 - zl, starts))):
+            c = j - d
+
+            @pl.when(jnp.logical_and(jnp.logical_not(last), jnp.logical_and(c >= 0, c < CHUNKS)))
+            def _():
+                wall_copy(way, wait_g[way], c).wait_recv()
+                wall_copy(way, send_g[way], c).start()
+
+    def pump_first():
+        for way, last in enumerate((ends, starts)):
+
+            @pl.when(last)
+            def _():
+                for c in range(CHUNKS):
+                    wall_copy(way, send_g[way], c).start()
+
+    def pump_last():
+        for way, last in enumerate((ends, starts)):
+
+            @pl.when(last)
+            def _():
+                for c in range(CHUNKS):
+                    wall_copy(way, wait_g[way], c).wait_recv()
 
     for i in range(1, NY):
         keep_copy(i).start()
     for i in range(1, NY):
         cut_copy(i).start()
     halo_copy(0).start()
-    for g in range(1, groups):
-        wall_copy(g).start()
+    own_w.wait()
+    pump_first()
+    pump(0)
 
     for i in range(1, NY):
         o = in_row(i)
@@ -210,8 +278,10 @@
     def halo_got(k):
         remote(halo.at[k - 1], halo.at[k], halo_s.at[k - 1], halo_r.at[k], at(pos, col)).wait_recv()
 
+    pump(1)
     halo_got(1)
     halo_copy(1).start()
+    pump(2)
 
     for i in range(1, nr):
         o = in_rows(i)
@@ -230,8 +300,10 @@
     for i in range(1, nr):
         ent_copy(i).start()
 
+    pump(3)
     halo_got(2)
     halo_copy(2).start()
+    pump(4)
 
     for i in range(1, nr):
         o = in_rows(i)
@@ -253,8 +325,10 @@
     for i in range(1, NY):
         back_copy(i).start()
 
+    pump(5)
     halo_got(3)
     halo_copy(3).start()
+    pump(6)
 
     for i in range(1, NY):
         o = in_row(i)
@@ -282,6 +356,7 @@
     for g in range(1, groups):
         read_copy(g).start()
 
+    pump(7)
     halo_got(4)
     scale = 1.0 / math.sqrt(HD)
     causal = lax.broadcasted_iota(jnp.int32, (HD, HD), 1) <= lax.broadcasted_iota(jnp.int32, (HD, HD), 0)
@@ -304,10 +379,11 @@
         vals = jnp.concatenate([halo[k, HD : 2 * HD, cols] for k in range(WMAX + 1)], 0)
         att_ref[:, cols] = dot(w, vals, 1, 0).astype(BF16)
 
-    own_w.wait()
+    for j in range(8, CHUNKS + NZ - 2):
+        pump(j)
+    pump_last()
     for g in range(1, groups):
         o = lax.rem(zh + g, groups)
-        remote(wo_ref, wall.at[o], wall_s.at[g], wall_r.at[o], at(pos, col)).wait_recv()
         remote(reads.at[o], reads.at[o], read_s.at[g], read_r.at[o], at(pos, col)).wait_recv()
     left = jnp.concatenate([reads[g] for g in range(groups)], 1)
 
@@ -334,8 +410,10 @@
     for k in range(WMAX):
         halo_copy(k).wait_send()
     for g in range(1, groups):
-        wall_copy(g).wait_send()
         read_copy(g).wait_send()
+    for c in range(CHUNKS):
+        for way in range(2):
+            wall_copy(way, send_g[way], c).wait_send()
     for c in range(n_out):
         part_copy(c).wait_send()
 
@@ -347,6 +425,7 @@
 
     def shards(queries, keys, values, memory_first, memory_second_weight, out_weight, decay, boundary, win_blocks):
         d = out_weight.shape[1]
+        hbm = pl.BlockSpec(memory_space=pltpu.HBM)
         vmem = pl.BlockSpec(memory_space=pltpu.VMEM)
         smem = pl.BlockSpec(memory_space=pltpu.SMEM)
         dma = pltpu.SemaphoreType.DMA
@@ -357,9 +436,13 @@
                     jax.ShapeDtypeStruct((HD, 2 * HD), BF16),
                     jax.ShapeDtypeStruct((HD, d), BF16),
                 ),
-                in_specs=[vmem] * 5 + [pl.BlockSpec(memory_space=pl.ANY)] + [vmem, smem, smem],
+                in_specs=[hbm] * 7 + [smem] * 2,
                 out_specs=(vmem, vmem),
                 scratch_shapes=[
+                    pltpu.VMEM((HD, 2 * HD), BF16),
+                    pltpu.VMEM((2, HD, MEM), BF16),
+                    pltpu.VMEM((2, MEM, HD), BF16),
+                    pltpu.VMEM((1, 2, MEM), F32),
                     pltpu.VMEM((WMAX + 1, 2 * HD + 16, 2 * HD), BF16),
                     pltpu.VMEM((NY, SUB, MEM), F32),
                     pltpu.VMEM((4, HD, MEM), F32),
@@ -376,6 +459,7 @@
                     pltpu.VMEM((groups, HD, 2 * HD), BF16),
                     pltpu.VMEM((d // OUT_COLS, HD, OUT_COLS), BF16),
                     pltpu.VMEM((d // OUT_COLS, HD, OUT_COLS), BF16),
+                    dma((6,)),
                     dma((WMAX + 1,)),
                     dma((WMAX + 1,)),
                     dma((NY,)),
@@ -388,8 +472,10 @@
                     dma((nr,)),
                     dma((NY,)),
                     dma((NY,)),
-                    dma((groups,)),
-                    dma((groups,)),
+                    dma((CHUNKS,)),
+                    dma((CHUNKS,)),
+                    dma((CHUNKS,)),
+                    dma((CHUNKS,)),
                     dma,
                     dma((groups,)),
                     dma((groups,)),
@@ -397,7 +483,7 @@
                     dma((d // OUT_COLS,)),
                 ],
                 compiler_params=pltpu.CompilerParams(
-                    collective_id=0, has_side_effects=True, vmem_limit_bytes=48 * 2**20
+                    collective_id=0, has_side_effects=True, vmem_limit_bytes=60 * 2**20
                 ),
             )(
                 queries,

time: 154 us -> 82.5 us (0.54)
  Pallas kernels: 144 us -> 76.8 us
  local copies, waits for them, and re-layouts: 7.65 us -> 3.35 us
    pallas_call x1, Pallas kernels: 144 us -> 76.8 us  [shards(): pl.pallas_call(functools.partial(kernel, n_stretch, n_col), out_shape=(ja...]
    unnamed x18 -> x2, local copies, waits for them, and re-layouts: 7.65 us -> 3.35 us
where the time goes in v2:
time: 82.5 us; the launch traced here: 81.4 us
  Pallas kernels  76.8 us (93%)
  local copies, waits for them, and re-layouts  3.35 us (4%)
  between operations  1.29 us (2%)
    pallas_call x1, Pallas kernels, shards(): pl.pallas_call(functools.partial(kernel, n_stretch, n_col), out_shape=(ja...  76.8 us
    unnamed x2, local copies, waits for them, and re-layouts  3.35 us

profile of v2, /device:TPU:1, one launch (start us, length us, event | category | flops | bytes accessed | tf_op | source)
XLA Modules:
  0.0 81.4 jit_solution(453835865578617389)
XLA Ops:
  1.3 76.8 %shard_map.104 = (bf16[128,256]{1,0:T(8,128)(2,1)}, bf16[128,2048]{1,0:T(8,128)(2,1)}) custom-call(bf16[128,256]{1,0:T(8,128)(2,1)} %q_hbm.1, bf16[128,256]{1,0:T(8,128)(2,1)} %k_hbm.1, bf16[128,256]{1,0:T(8,128)(2,1)} %v_hbm.1, bf16[2,128,256]{2,1,0:T(8,128)(2,1)} %m1_hbm.1, bf16[2,256,128]{2,1,0:T(8,128)(2,1)} %m2_hbm.1, bf16[256,2048]{1,0:T(8,128)(2,1)} %wo_ref.1, ...), custom_call_target="tpu_custom_call" | custom-call | tf_op jit(solution)/shard_map/pallas_call | solution.py:433
  78.1 1.5 %copy.14 = bf16[128,256]{1,0:T(8,128)(2,1)} copy(bf16[128,256]{1,0:T(8,128)(2,1)} %get-tuple-element.4) | data formatting | bytes 131072
  79.6 1.9 %copy.15 = bf16[128,2048]{1,0:T(8,128)(2,1)} copy(bf16[128,2048]{1,0:T(8,128)(2,1)} %get-tuple-element.5) | data formatting | bytes 1048576

commit v3 on v2

--- a/solution.py
+++ b/solution.py
@@ -13,7 +13,9 @@
 WMAX = 4
 NY = 8
 NZ = 4
-CHUNKS = 8
+DIRECT = 128
+PARTS = 5
+DUE = (((0, 1), (2, 3), (4,), ()), ((0,), (1, 2), (3,), (4,)), ((), (0,), (1, 2), (3, 4)), ((), (), (), ()))
 LANES = 128
 SUB = 8
 OUT_COLS = 512
@@ -36,14 +38,15 @@
     m2_hbm,
     wo_ref,
     decay_hbm,
+    win_hbm,
     bnd_ref,
-    win_ref,
     att_ref,
     out_ref,
     q_ref,
     m1_ref,
     m2_ref,
     decay_ref,
+    win_ref,
     halo,
     keeps,
     upd,
@@ -77,6 +80,8 @@
     up_r,
     down_s,
     down_r,
+    across_s,
+    across_r,
     wall_l,
     read_s,
     read_r,
@@ -84,6 +89,7 @@
     part_r,
 ):
     nr = n_stretch // NY
+    nx = nr // NZ
     groups = n_col // 2
     sr = HD // NY
     dh_n = sr // SUB
@@ -95,6 +101,7 @@
     y = lax.rem(pos, NY)
     r = pos // NY
     zl = lax.rem(r, NZ)
+    xs = r // NZ
     zh = col // 2
     core = lax.rem(col, 2)
     after = lax.rem(pos + 1, n_stretch)
@@ -152,6 +159,7 @@
                 (v_hbm, own.at[HD : 2 * HD]),
                 (decay_hbm, decay_ref),
                 (q_hbm, q_ref),
+                (win_hbm, win_ref),
             )
         )
     ]
@@ -159,10 +167,10 @@
         load.start()
     own_w = pltpu.make_async_copy(wo_ref, wall.at[zh], wall_l)
     own_w.start()
+    for load in loads:
+        load.wait()
     flag = bnd_ref[0].astype(F32)
     halo[0, 2 * HD :, :] = jnp.full((16, 2 * HD), flag, F32).astype(BF16)
-    for load in loads:
-        load.wait()
     keep2 = decay_ref[0] * (1.0 - flag)
     keeps[y] = jnp.concatenate([keep2, jnp.zeros((SUB - 2, MEM), F32)], 0)
 
@@ -196,45 +204,74 @@
     def halo_copy(k):
         return remote(halo.at[k], halo.at[k + 1], halo_s.at[k], halo_r.at[k + 1], at(after, col))
 
-    rows_c = 2 * HD // CHUNKS
+    rows_x = (2 * HD - DIRECT) // nx
+    rows_c = DIRECT // (PARTS - 1)
     wait_g = lax.rem(zh + groups - 1, groups), lax.rem(zh + 1, groups)
     send_g = jnp.where(ends, zh, wait_g[0]), jnp.where(starts, zh, wait_g[1])
+    chain = zl, NZ - 1 - zl
+
+    def share(g, xx):
+        return wall.at[g, pl.ds(pl.multiple_of(DIRECT + xx * rows_x, rows_x), rows_x)]
 
     def wall_copy(way, g, c):
-        piece = wall.at[g, pl.ds(pl.multiple_of(c * rows_c, rows_c), rows_c)]
+        piece = share(g, xs) if c == 0 else wall.at[g, (c - 1) * rows_c : c * rows_c]
         sem_s, sem_r = ((up_s, up_r), (down_s, down_r))[way]
         return remote(piece, piece, sem_s.at[c], sem_r.at[c], (above, below)[way])
 
-    def pump(j):
-        for way, (d, last) in enumerate(((zl, ends), (NZ - 1 - zl, starts))):
-            c = j - d
-
-            @pl.when(jnp.logical_and(jnp.logical_not(last), jnp.logical_and(c >= 0, c < CHUNKS)))
+    def across_copy(way, i):
+        piece = share(wait_g[way], xs)
+        to = lax.rem(pos + i * NY * NZ, n_stretch)
+        return remote(piece, piece, across_s.at[way, i], across_r.at[way, i], at(to, col))
+
+    def across_got(way, i):
+        piece = share(wait_g[way], lax.rem(xs + nx - i, nx))
+        remote(piece, piece, across_s.at[way, i], across_r.at[way, i], at(pos, col)).wait_recv()
+
+    def took(way, c):
+        wall_copy(way, wait_g[way], c).wait_recv()
+        if c == 0:
+            for i in range(1, nx):
+                across_copy(way, i).start()
+
+    def pump(point):
+        for way in range(2):
+            for d in range(NZ - 1):
+
+                @pl.when(chain[way] == d)
+                def _():
+                    for c in DUE[d][point]:
+                        took(way, c)
+                        wall_copy(way, send_g[way], c).start()
+
+            if point == 2:
+
+                @pl.when(chain[way] == NZ - 1)
+                def _():
+                    took(way, 0)
+
+    def pump_first():
+        for c in range(PARTS):
+            for way in range(2):
+
+                @pl.when(chain[way] == NZ - 1)
+                def _():
+                    wall_copy(way, zh, c).start()
+
+    def pump_last():
+        for way in range(2):
+
+            @pl.when(chain[way] == NZ - 1)
             def _():
-                wall_copy(way, wait_g[way], c).wait_recv()
-                wall_copy(way, send_g[way], c).start()
-
-    def pump_first():
-        for way, last in enumerate((ends, starts)):
-
-            @pl.when(last)
-            def _():
-                for c in range(CHUNKS):
-                    wall_copy(way, send_g[way], c).start()
-
-    def pump_last():
-        for way, last in enumerate((ends, starts)):
-
-            @pl.when(last)
-            def _():
-                for c in range(CHUNKS):
-                    wall_copy(way, wait_g[way], c).wait_recv()
+                for c in range(1, PARTS):
+                    took(way, c)
+
+            for i in range(1, nx):
+                across_got(way, i)
 
     for i in range(1, NY):
         keep_copy(i).start()
     for i in range(1, NY):
         cut_copy(i).start()
-    halo_copy(0).start()
     own_w.wait()
     pump_first()
     pump(0)
@@ -278,10 +315,8 @@
     def halo_got(k):
         remote(halo.at[k - 1], halo.at[k], halo_s.at[k - 1], halo_r.at[k], at(pos, col)).wait_recv()
 
+    halo_copy(0).start()
     pump(1)
-    halo_got(1)
-    halo_copy(1).start()
-    pump(2)
 
     for i in range(1, nr):
         o = in_rows(i)
@@ -300,10 +335,9 @@
     for i in range(1, nr):
         ent_copy(i).start()
 
-    pump(3)
-    halo_got(2)
-    halo_copy(2).start()
-    pump(4)
+    halo_got(1)
+    halo_copy(1).start()
+    pump(2)
 
     for i in range(1, nr):
         o = in_rows(i)
@@ -325,10 +359,9 @@
     for i in range(1, NY):
         back_copy(i).start()
 
-    pump(5)
-    halo_got(3)
-    halo_copy(3).start()
-    pump(6)
+    halo_got(2)
+    halo_copy(2).start()
+    pump(3)
 
     for i in range(1, NY):
         o = in_row(i)
@@ -356,7 +389,8 @@
     for g in range(1, groups):
         read_copy(g).start()
 
-    pump(7)
+    halo_got(3)
+    halo_copy(3).start()
     halo_got(4)
     scale = 1.0 / math.sqrt(HD)
     causal = lax.broadcasted_iota(jnp.int32, (HD, HD), 1) <= lax.broadcasted_iota(jnp.int32, (HD, HD), 0)
@@ -379,8 +413,6 @@
         vals = jnp.concatenate([halo[k, HD : 2 * HD, cols] for k in range(WMAX + 1)], 0)
         att_ref[:, cols] = dot(w, vals, 1, 0).astype(BF16)
 
-    for j in range(8, CHUNKS + NZ - 2):
-        pump(j)
     pump_last()
     for g in range(1, groups):
         o = lax.rem(zh + g, groups)
@@ -411,9 +443,11 @@
         halo_copy(k).wait_send()
     for g in range(1, groups):
         read_copy(g).wait_send()
-    for c in range(CHUNKS):
-        for way in range(2):
+    for way in range(2):
+        for c in range(PARTS):
             wall_copy(way, send_g[way], c).wait_send()
+        for i in range(1, nx):
+            across_copy(way, i).wait_send()
     for c in range(n_out):
         part_copy(c).wait_send()
 
@@ -427,7 +461,6 @@
         d = out_weight.shape[1]
         hbm = pl.BlockSpec(memory_space=pltpu.HBM)
         vmem = pl.BlockSpec(memory_space=pltpu.VMEM)
-        smem = pl.BlockSpec(memory_space=pltpu.SMEM)
         dma = pltpu.SemaphoreType.DMA
         return tuple(
             pl.pallas_call(
@@ -436,13 +469,14 @@
                     jax.ShapeDtypeStruct((HD, 2 * HD), BF16),
                     jax.ShapeDtypeStruct((HD, d), BF16),
                 ),
-                in_specs=[hbm] * 7 + [smem] * 2,
+                in_specs=[hbm] * 8 + [pl.BlockSpec(memory_space=pltpu.SMEM)],
                 out_specs=(vmem, vmem),
                 scratch_shapes=[
                     pltpu.VMEM((HD, 2 * HD), BF16),
                     pltpu.VMEM((2, HD, MEM), BF16),
                     pltpu.VMEM((2, MEM, HD), BF16),
                     pltpu.VMEM((1, 2, MEM), F32),
+                    pltpu.SMEM((2,), jnp.int32),
                     pltpu.VMEM((WMAX + 1, 2 * HD + 16, 2 * HD), BF16),
                     pltpu.VMEM((NY, SUB, MEM), F32),
                     pltpu.VMEM((4, HD, MEM), F32),
@@ -459,7 +493,7 @@
                     pltpu.VMEM((groups, HD, 2 * HD), BF16),
                     pltpu.VMEM((d // OUT_COLS, HD, OUT_COLS), BF16),
                     pltpu.VMEM((d // OUT_COLS, HD, OUT_COLS), BF16),
-                    dma((6,)),
+                    dma((7,)),
                     dma((WMAX + 1,)),
                     dma((WMAX + 1,)),
                     dma((NY,)),
@@ -472,10 +506,12 @@
                     dma((nr,)),
                     dma((NY,)),
                     dma((NY,)),
-                    dma((CHUNKS,)),
-                    dma((CHUNKS,)),
-                    dma((CHUNKS,)),
-                    dma((CHUNKS,)),
+                    dma((PARTS,)),
+                    dma((PARTS,)),
+                    dma((PARTS,)),
+                    dma((PARTS,)),
+                    dma((2, nr // NZ)),
+                    dma((2, nr // NZ)),
                     dma,
                     dma((groups,)),
                     dma((groups,)),
@@ -483,18 +519,23 @@
                     dma((d // OUT_COLS,)),
                 ],
                 compiler_params=pltpu.CompilerParams(
-                    collective_id=0, has_side_effects=True, vmem_limit_bytes=60 * 2**20
+                    collective_id=0, has_side_effects=True, vmem_limit_bytes=48 * 2**20
                 ),
             )(
-                queries,
-                keys,
-                values,
-                memory_first,
-                memory_second_weight,
-                out_weight,
-                decay,
+                *(
+                    pltpu.with_memory_space_constraint(x, pltpu.HBM)
+                    for x in (
+                        queries,
+                        keys,
+                        values,
+                        memory_first,
+                        memory_second_weight,
+                        out_weight,
+                        decay,
+                        win_blocks,
+                    )
+                ),
                 boundary,
-                win_blocks,
             )
         )
 

time: 82.5 us -> 74.9 us (0.908)
  Pallas kernels: 76.8 us -> 71 us
  local copies, waits for them, and re-layouts: 3.35 us -> 1.42 us
    pallas_call x1, Pallas kernels: 76.8 us -> 71 us  [shards(): pl.pallas_call(functools.partial(kernel, n_stretch, n_col), out_shape=(ja...]
    unnamed x2, local copies, waits for them, and re-layouts: 3.35 us -> 1.42 us
where the time goes in v3:
time: 74.9 us; the launch traced here: 73.7 us
  Pallas kernels  71 us (95%)
  local copies, waits for them, and re-layouts  1.42 us (2%)
  between operations  1.29 us (2%)
    pallas_call x1, Pallas kernels, shards(): pl.pallas_call(functools.partial(kernel, n_stretch, n_col), out_shape=(ja...  71 us

profile of v3, /device:TPU:1, one launch (start us, length us, event | category | flops | bytes accessed | tf_op | source)
XLA Modules:
  0.0 73.7 jit_solution(367324269617497953)
XLA Ops:
  1.3 71.0 %shard_map.104 = (bf16[128,256]{1,0:T(8,128)(2,1)S(1)}, bf16[128,2048]{1,0:T(8,128)(2,1)S(1)}) custom-call(bf16[128,256]{1,0:T(8,128)(2,1)} %q_hbm.1, bf16[128,256]{1,0:T(8,128)(2,1)} %k_hbm.1, bf16[128,256]{1,0:T(8,128)(2,1)} %v_hbm.1, bf16[2,128,256]{2,1,0:T(8,128)(2,1)} %m1_hbm.1, bf16[2,256,128]{2,1,0:T(8,128)(2,1)} %m2_hbm.1, bf16[256,2048]{1,0:T(8,128)(2,1)} %wo_ref.1, ...), custom_call_target="tpu_custom_call" | custom-call | tf_op jit(solution)/shard_map/pallas_call | solution.py:466
  72.2 0.6 copy.14
  72.9 0.8 %copy.15 = bf16[128,2048]{1,0:T(8,128)(2,1)} copy(bf16[128,2048]{1,0:T(8,128)(2,1)S(1)} %get-tuple-element.5) | data formatting | bytes 1048576

commit v4 on v3

--- a/solution.py
+++ b/solution.py
@@ -13,9 +13,8 @@
 WMAX = 4
 NY = 8
 NZ = 4
-DIRECT = 128
-PARTS = 5
-DUE = (((0, 1), (2, 3), (4,), ()), ((0,), (1, 2), (3,), (4,)), ((), (0,), (1, 2), (3, 4)), ((), (), (), ()))
+PARTS = 2
+DUE = (((0, 1), (), ()), ((0,), (1,), ()), ((), (0,), (1,)), ((), (), (0, 1)))
 LANES = 128
 SUB = 8
 OUT_COLS = 512
@@ -104,8 +103,6 @@
     xs = r // NZ
     zh = col // 2
     core = lax.rem(col, 2)
-    after = lax.rem(pos + 1, n_stretch)
-    before = lax.rem(pos + n_stretch - 1, n_stretch)
     sibling = col + 1 - 2 * core
 
     def at(s, c):
@@ -139,14 +136,14 @@
         greet(at(r * NY + in_row(i), col))
     for i in range(1, nr):
         greet(at(in_rows(i) * NY + y, col))
-    greet(at(after, col))
-    greet(at(before, col))
+    for i in (1, 2, n_stretch - 1, n_stretch - 2):
+        greet(at(lax.rem(pos + i, n_stretch), col))
     for g in range(1, groups):
         greet(at(pos, lax.rem(col + 2 * g, n_col)))
     greet(at(pos, sibling))
     greet(above)
     greet(below)
-    greeted = (NY - 1) + (nr - 1) + 2 + (groups - 1) + 1 + 2
+    greeted = (NY - 1) + (nr - 1) + 4 + (groups - 1) + 1 + 2
 
     own = halo.at[0]
     loads = [
@@ -201,72 +198,58 @@
         to = in_row(i)
         return remote(cut.at[to], got.at[y], cut_s.at[to], cut_r.at[y], at(r * NY + to, col))
 
-    def halo_copy(k):
-        return remote(halo.at[k], halo.at[k + 1], halo_s.at[k], halo_r.at[k + 1], at(after, col))
-
-    rows_x = (2 * HD - DIRECT) // nx
-    rows_c = DIRECT // (PARTS - 1)
+    def halo_copy(k, ahead):
+        to = lax.rem(pos + ahead, n_stretch)
+        return remote(halo.at[k], halo.at[k + ahead], halo_s.at[k + ahead - 1], halo_r.at[k + ahead], at(to, col))
+
+    rows_c = 2 * HD // nx // PARTS
     wait_g = lax.rem(zh + groups - 1, groups), lax.rem(zh + 1, groups)
     send_g = jnp.where(ends, zh, wait_g[0]), jnp.where(starts, zh, wait_g[1])
     chain = zl, NZ - 1 - zl
 
-    def share(g, xx):
-        return wall.at[g, pl.ds(pl.multiple_of(DIRECT + xx * rows_x, rows_x), rows_x)]
+    def share(g, xx, c):
+        return wall.at[g, pl.ds(pl.multiple_of((xx * PARTS + c) * rows_c, rows_c), rows_c)]
 
     def wall_copy(way, g, c):
-        piece = share(g, xs) if c == 0 else wall.at[g, (c - 1) * rows_c : c * rows_c]
+        piece = share(g, xs, c)
         sem_s, sem_r = ((up_s, up_r), (down_s, down_r))[way]
         return remote(piece, piece, sem_s.at[c], sem_r.at[c], (above, below)[way])
 
-    def across_copy(way, i):
-        piece = share(wait_g[way], xs)
+    def across_copy(way, c, i):
+        piece = share(wait_g[way], xs, c)
         to = lax.rem(pos + i * NY * NZ, n_stretch)
-        return remote(piece, piece, across_s.at[way, i], across_r.at[way, i], at(to, col))
-
-    def across_got(way, i):
-        piece = share(wait_g[way], lax.rem(xs + nx - i, nx))
-        remote(piece, piece, across_s.at[way, i], across_r.at[way, i], at(pos, col)).wait_recv()
-
-    def took(way, c):
-        wall_copy(way, wait_g[way], c).wait_recv()
-        if c == 0:
-            for i in range(1, nx):
-                across_copy(way, i).start()
+        return remote(piece, piece, across_s.at[way, c, i], across_r.at[way, c, i], at(to, col))
+
+    def across_got(way, c, i):
+        piece = share(wait_g[way], lax.rem(xs + nx - i, nx), c)
+        remote(piece, piece, across_s.at[way, c, i], across_r.at[way, c, i], at(pos, col)).wait_recv()
 
     def pump(point):
         for way in range(2):
-            for d in range(NZ - 1):
+            for d in range(NZ):
 
                 @pl.when(chain[way] == d)
                 def _():
                     for c in DUE[d][point]:
-                        took(way, c)
-                        wall_copy(way, send_g[way], c).start()
-
-            if point == 2:
-
-                @pl.when(chain[way] == NZ - 1)
-                def _():
-                    took(way, 0)
+                        wall_copy(way, wait_g[way], c).wait_recv()
+                        if d < NZ - 1:
+                            wall_copy(way, send_g[way], c).start()
+                        for i in range(1, nx):
+                            across_copy(way, c, i).start()
 
     def pump_first():
-        for c in range(PARTS):
-            for way in range(2):
-
-                @pl.when(chain[way] == NZ - 1)
-                def _():
+        for way in range(2):
+
+            @pl.when(chain[way] == NZ - 1)
+            def _():
+                for c in range(PARTS):
                     wall_copy(way, zh, c).start()
 
     def pump_last():
         for way in range(2):
-
-            @pl.when(chain[way] == NZ - 1)
-            def _():
-                for c in range(1, PARTS):
-                    took(way, c)
-
-            for i in range(1, nx):
-                across_got(way, i)
+            for c in range(PARTS):
+                for i in range(1, nx):
+                    across_got(way, c, i)
 
     for i in range(1, NY):
         keep_copy(i).start()
@@ -274,7 +257,6 @@
         cut_copy(i).start()
     own_w.wait()
     pump_first()
-    pump(0)
 
     for i in range(1, NY):
         o = in_row(i)
@@ -313,10 +295,11 @@
         tot_copy(i).start()
 
     def halo_got(k):
-        remote(halo.at[k - 1], halo.at[k], halo_s.at[k - 1], halo_r.at[k], at(pos, col)).wait_recv()
-
-    halo_copy(0).start()
-    pump(1)
+        remote(halo.at[0], halo.at[k], halo_s.at[k - 1], halo_r.at[k], at(pos, col)).wait_recv()
+
+    halo_copy(0, 2).start()
+    halo_copy(0, 1).start()
+    pump(0)
 
     for i in range(1, nr):
         o = in_rows(i)
@@ -335,9 +318,7 @@
     for i in range(1, nr):
         ent_copy(i).start()
 
-    halo_got(1)
-    halo_copy(1).start()
-    pump(2)
+    pump(1)
 
     for i in range(1, nr):
         o = in_rows(i)
@@ -359,9 +340,7 @@
     for i in range(1, NY):
         back_copy(i).start()
 
-    halo_got(2)
-    halo_copy(2).start()
-    pump(3)
+    pump(2)
 
     for i in range(1, NY):
         o = in_row(i)
@@ -389,8 +368,25 @@
     for g in range(1, groups):
         read_copy(g).start()
 
+    halo_got(2)
+    halo_copy(2, 2).start()
+    halo_copy(2, 1).start()
+    pump_last()
+    for g in range(1, groups):
+        o = lax.rem(zh + g, groups)
+        remote(reads.at[o], reads.at[o], read_s.at[g], read_r.at[o], at(pos, col)).wait_recv()
+    left = jnp.concatenate([reads[g] for g in range(groups)], 1)
+
+    def part_copy(c):
+        return remote(part.at[c], part_in.at[c], part_s.at[c], part_r.at[c], at(pos, sibling))
+
+    for c in range(n_out):
+        cs = slice(c * OUT_COLS, (c + 1) * OUT_COLS)
+        right = jnp.concatenate([wall[g, :, cs] for g in range(groups)], 0)
+        part[c] = dot(left, right, 1, 0).astype(BF16)
+        part_copy(c).start()
+    halo_got(1)
     halo_got(3)
-    halo_copy(3).start()
     halo_got(4)
     scale = 1.0 / math.sqrt(HD)
     causal = lax.broadcasted_iota(jnp.int32, (HD, HD), 1) <= lax.broadcasted_iota(jnp.int32, (HD, HD), 0)
@@ -413,20 +409,6 @@
         vals = jnp.concatenate([halo[k, HD : 2 * HD, cols] for k in range(WMAX + 1)], 0)
         att_ref[:, cols] = dot(w, vals, 1, 0).astype(BF16)
 
-    pump_last()
-    for g in range(1, groups):
-        o = lax.rem(zh + g, groups)
-        remote(reads.at[o], reads.at[o], read_s.at[g], read_r.at[o], at(pos, col)).wait_recv()
-    left = jnp.concatenate([reads[g] for g in range(groups)], 1)
-
-    def part_copy(c):
-        return remote(part.at[c], part_in.at[c], part_s.at[c], part_r.at[c], at(pos, sibling))
-
-    for c in range(n_out):
-        cs = slice(c * OUT_COLS, (c + 1) * OUT_COLS)
-        right = jnp.concatenate([wall[g, :, cs] for g in range(groups)], 0)
-        part[c] = dot(left, right, 1, 0).astype(BF16)
-        part_copy(c).start()
     for c in range(n_out):
         cs = slice(c * OUT_COLS, (c + 1) * OUT_COLS)
         part_copy(c).wait_recv()
@@ -439,15 +421,16 @@
     for i in range(1, nr):
         tot_copy(i).wait_send()
         ent_copy(i).wait_send()
-    for k in range(WMAX):
-        halo_copy(k).wait_send()
+    for k in (0, 2):
+        for ahead in (1, 2):
+            halo_copy(k, ahead).wait_send()
     for g in range(1, groups):
         read_copy(g).wait_send()
     for way in range(2):
         for c in range(PARTS):
             wall_copy(way, send_g[way], c).wait_send()
-        for i in range(1, nx):
-            across_copy(way, i).wait_send()
+            for i in range(1, nx):
+                across_copy(way, c, i).wait_send()
     for c in range(n_out):
         part_copy(c).wait_send()
 
@@ -510,8 +493,8 @@
                     dma((PARTS,)),
                     dma((PARTS,)),
                     dma((PARTS,)),
-                    dma((2, nr // NZ)),
-                    dma((2, nr // NZ)),
+                    dma((2, PARTS, nr // NZ)),
+                    dma((2, PARTS, nr // NZ)),
                     dma,
                     dma((groups,)),
                     dma((groups,)),

time: 74.9 us -> 72.9 us (0.973); the launches traced: 73.7 us -> 72.7 us
  Pallas kernels: 71 us -> 70 us
    pallas_call x1, Pallas kernels: 71 us -> 70 us  [shards(): pl.pallas_call(functools.partial(kernel, n_stretch, n_col), out_shape=(ja...]
where the time goes in v4:
time: 72.9 us; the launch traced here: 72.7 us
  Pallas kernels  70 us (96%)
  local copies, waits for them, and re-layouts  1.42 us (2%)
  between operations  1.29 us (2%)
    pallas_call x1, Pallas kernels, shards(): pl.pallas_call(functools.partial(kernel, n_stretch, n_col), out_shape=(ja...  70 us

profile of v4, /device:TPU:1, one launch (start us, length us, event | category | flops | bytes accessed | tf_op | source)
XLA Modules:
  0.0 72.7 jit_solution(10075260723737819067)
XLA Ops:
  1.3 70.0 %shard_map.104 = (bf16[128,256]{1,0:T(8,128)(2,1)S(1)}, bf16[128,2048]{1,0:T(8,128)(2,1)S(1)}) custom-call(bf16[128,256]{1,0:T(8,128)(2,1)} %q_hbm.1, bf16[128,256]{1,0:T(8,128)(2,1)} %k_hbm.1, bf16[128,256]{1,0:T(8,128)(2,1)} %v_hbm.1, bf16[2,128,256]{2,1,0:T(8,128)(2,1)} %m1_hbm.1, bf16[2,256,128]{2,1,0:T(8,128)(2,1)} %m2_hbm.1, bf16[256,2048]{1,0:T(8,128)(2,1)} %wo_ref.1, ...), custom_call_target="tpu_custom_call" | custom-call | tf_op jit(solution)/shard_map/pallas_call | solution.py:449
  71.3 0.6 copy.14
  71.9 0.8 %copy.15 = bf16[128,2048]{1,0:T(8,128)(2,1)} copy(bf16[128,2048]{1,0:T(8,128)(2,1)S(1)} %get-tuple-element.5) | data formatting | bytes 1048576

commit v5 on v4

--- a/solution.py
+++ b/solution.py
@@ -298,7 +298,6 @@
         remote(halo.at[0], halo.at[k], halo_s.at[k - 1], halo_r.at[k], at(pos, col)).wait_recv()
 
     halo_copy(0, 2).start()
-    halo_copy(0, 1).start()
     pump(0)
 
     for i in range(1, nr):
@@ -371,6 +370,7 @@
     halo_got(2)
     halo_copy(2, 2).start()
     halo_copy(2, 1).start()
+    halo_copy(0, 1).start()
     pump_last()
     for g in range(1, groups):
         o = lax.rem(zh + g, groups)

time: 72.9 us -> 72.6 us (level)
  the two profiles are of different devices: /device:TPU:1 before, /device:TPU:57 now
where the time goes in v5:
time: 72.6 us; the launch traced here: 72.5 us
  Pallas kernels  69.8 us (96%)
  local copies, waits for them, and re-layouts  1.42 us (2%)
  between operations  1.29 us (2%)
    pallas_call x1, Pallas kernels, shards(): pl.pallas_call(functools.partial(kernel, n_stretch, n_col), out_shape=(ja...  69.8 us

profile of v5, /device:TPU:57, one launch (start us, length us, event | category | flops | bytes accessed | tf_op | source)
XLA Modules:
  0.0 72.5 jit_solution(14055961737129433963)
XLA Ops:
  1.3 69.8 %shard_map.104 = (bf16[128,256]{1,0:T(8,128)(2,1)S(1)}, bf16[128,2048]{1,0:T(8,128)(2,1)S(1)}) custom-call(bf16[128,256]{1,0:T(8,128)(2,1)} %q_hbm.1, bf16[128,256]{1,0:T(8,128)(2,1)} %k_hbm.1, bf16[128,256]{1,0:T(8,128)(2,1)} %v_hbm.1, bf16[2,128,256]{2,1,0:T(8,128)(2,1)} %m1_hbm.1, bf16[2,256,128]{2,1,0:T(8,128)(2,1)} %m2_hbm.1, bf16[256,2048]{1,0:T(8,128)(2,1)} %wo_ref.1, ...), custom_call_target="tpu_custom_call" | custom-call | tf_op jit(solution)/shard_map/pallas_call | solution.py:449
  71.0 0.6 copy.14
  71.7 0.8 %copy.15 = bf16[128,2048]{1,0:T(8,128)(2,1)} copy(bf16[128,2048]{1,0:T(8,128)(2,1)S(1)} %get-tuple-element.5) | data formatting | bytes 1048576
